TPU v7x, 128 devices: a whole 4x4x4 slice. The times are simulated.
128 devices in a mesh: rows: 32 (over x_hi, y, z), text: 4 (over x_lo, core).
Axes of the slice: x: 4 (x_hi: 2, x_lo: 2; x = x_hi * 2 + x_lo), y: 4, z: 4, core: 2. Of those that a mesh axis runs over, the one named last changes fastest.
Arguments:
- image_tokens: bfloat16 [32, 512, 2048], P('rows', 'text'), may hold values from -6 to 6
- caption_embed: bfloat16 [32, 32, 4096], P('rows', 'text'), may hold values from -6 to 6
- caption_lengths: int32 [32, 2], P('rows'), may hold values from 5 to 16, as said below
- output_grad: bfloat16 [32, 512, 2048], P('rows', 'text'), may hold values from -6 to 6
- norm_self: bfloat16 [2048], P('rows'), may hold values from 0.5 to 1.5
- norm_cross: bfloat16 [2048], P('rows'), may hold values from 0.5 to 1.5
- norm_feed: bfloat16 [2048], P('rows'), may hold values from 0.5 to 1.5
- self_query: bfloat16 [2048, 2048], P('rows', 'text'), may hold values from -0.125 to 0.125
- self_key: bfloat16 [2048, 2048], P('rows', 'text'), may hold values from -0.125 to 0.125
- self_value: bfloat16 [2048, 2048], P('rows', 'text'), may hold values from -0.125 to 0.125
- self_output: bfloat16 [2048, 2048], P('text', 'rows'), may hold values from -1.5 to 1.5
- cross_query: bfloat16 [2048, 2048], P('rows', 'text'), may hold values from -0.125 to 0.125
- cross_key: bfloat16 [4096, 2048], P('rows', 'text'), may hold values from -0.09375 to 0.09375
- cross_value: bfloat16 [4096, 2048], P('rows', 'text'), may hold values from -0.09375 to 0.09375
- cross_output: bfloat16 [2048, 2048], P('text', 'rows'), may hold values from -0.375 to 0.375
- up_weight: bfloat16 [2048, 8192], P('rows', 'text'), may hold values from -0.125 to 0.125
- down_weight: bfloat16 [8192, 2048], P('text', 'rows'), may hold values from -0.0625 to 0.0625
Outputs:
- layer_output_array: bfloat16 [32, 512, 2048], P('rows', 'text')
- image_grad: float32 [32, 512, 2048], P('rows', 'text')
- caption_grad: float32 [32, 32, 4096], P('rows', 'text')
- norm_self_grad: float32 [2048], P('rows')
- norm_cross_grad: float32 [2048], P('rows')
- norm_feed_grad: float32 [2048], P('rows')
- self_query_grad: float32 [2048, 2048], P('rows', 'text')
- self_key_grad: float32 [2048, 2048], P('rows', 'text')
- self_value_grad: float32 [2048, 2048], P('rows', 'text')
- self_output_grad: float32 [2048, 2048], P('text', 'rows')
- cross_query_grad: float32 [2048, 2048], P('rows', 'text')
- cross_key_grad: float32 [4096, 2048], P('rows', 'text')
- cross_value_grad: float32 [4096, 2048], P('rows', 'text')
- cross_output_grad: float32 [2048, 2048], P('text', 'rows')
- up_grad: float32 [2048, 8192], P('rows', 'text')
- down_grad: float32 [8192, 2048], P('text', 'rows')
Inputs may be any that keep to these rules, and one draw needn't show every extreme that they name: caption_lengths[r, i] counts the live slots of image i's caption; slots at or past it are padding. Some image has 16 live slots and some has 5.
All inputs are finite; a program needn't handle non-finite values.
Results may differ from a plain program's by a relative error of at most 0.029.
Values may be sent and summed in bfloat16 or wider, within the bound.
No kernel may reach another device: no remote copies, remote signals or barrier semaphores. Data moves between devices by JAX's collectives and lax.ppermute only.
A program may use at most 192 MiB of HBM per device.

v0:
```python
import jax
import jax.numpy as jnp
from jax import lax
from jax.sharding import PartitionSpec as P

HEAD_DIM = 128
IMAGE_TOKENS = 256
PER_ROW = 2
CAP = 16
EPSILON = 1e-05


def layer_stats(resid):
    mean = jnp.mean(resid, -1, keepdims=True)
    centered = resid - mean
    inverse = lax.rsqrt(jnp.mean(centered * centered, -1, keepdims=True) + EPSILON)
    return (centered * inverse, inverse)


def norm_back(grad_norm, normed, inverse, gain):
    scaled = grad_norm * gain
    inner = (
        scaled
        - jnp.mean(scaled, -1, keepdims=True)
        - normed * jnp.mean(scaled * normed, -1, keepdims=True)
    )
    return (inverse * inner, jnp.sum(grad_norm * normed, axis=(0, 1)))


def gelu_back(hidden_pre, grad_act):
    _, pullback = jax.vjp(lambda value_in: jax.nn.gelu(value_in, approximate=False), hidden_pre)
    return pullback(grad_act)[0]


def gather_tokens(normed_low):
    return lax.all_gather(normed_low, "text", axis=1, tiled=True)


def sum_tokens(partial_value):
    return lax.psum_scatter(partial_value, "text", scatter_dimension=1, tiled=True)


def gather_grads(grad_low):
    return lax.all_gather(grad_low, "text", axis=1, tiled=True)


def sum_inputs(partial_value):
    return lax.psum_scatter(
        partial_value.astype(jnp.bfloat16), "text", scatter_dimension=1, tiled=True
    ).astype(jnp.float32)


def product(operand, factor):
    return jnp.einsum("rsd,de->rse", operand, factor, preferred_element_type=jnp.float32)


def project(operand, factor):
    return product(operand, factor).astype(jnp.bfloat16)


def product_back(operand, factor):
    return jnp.einsum("rse,de->rsd", operand, factor, preferred_element_type=jnp.float32)


def contract_product(operand, factor):
    return jnp.einsum("rsd,rse->de", operand, factor, preferred_element_type=jnp.float32)


def split_heads(value_rows, length_limit):
    return value_rows.reshape(
        value_rows.shape[0], PER_ROW, length_limit, value_rows.shape[2] // HEAD_DIM, HEAD_DIM
    )


def join_heads(value_rows):
    shape = value_rows.shape
    return value_rows.reshape(shape[0], shape[1] * shape[2], shape[3] * shape[4])


def scores_of(query_rows, key_rows):
    return jnp.einsum(
        "rbqhe,rbkhe->rbhqk", query_rows, key_rows, preferred_element_type=jnp.float32
    ) * HEAD_DIM ** (-0.5)


def attend_forward(query_rows, key_rows, value_rows, live_slots):
    scores = scores_of(query_rows, key_rows)
    if live_slots is not None:
        scores = jnp.where(live_slots, scores, -1e30)
    row_max = jnp.max(scores, -1, keepdims=True)
    shifted = jnp.exp(scores - row_max)
    row_total = jnp.sum(shifted, -1, keepdims=True)
    attention = (shifted / row_total).astype(jnp.bfloat16)
    mixed = jnp.einsum(
        "rbhqk,rbkhe->rbqhe", attention, value_rows, preferred_element_type=jnp.float32
    )
    return (mixed.astype(jnp.bfloat16), row_max + jnp.log(row_total))


def attend_back(query_rows, key_rows, value_rows, live_slots, logsum, grad_mixed):
    scores = scores_of(query_rows, key_rows)
    attention = jnp.exp(scores - logsum)
    if live_slots is not None:
        attention = jnp.where(live_slots, attention, 0.0)
    grad_values = jnp.einsum(
        "rbhqk,rbqhe->rbkhe",
        attention.astype(jnp.bfloat16),
        grad_mixed,
        preferred_element_type=jnp.float32,
    ).astype(jnp.bfloat16)
    grad_attention = jnp.einsum(
        "rbqhe,rbkhe->rbhqk", grad_mixed, value_rows, preferred_element_type=jnp.float32
    )
    row_inner = jnp.sum(attention * grad_attention, -1, keepdims=True)
    grad_scores = (attention * (grad_attention - row_inner)).astype(jnp.bfloat16)
    grad_query = (
        jnp.einsum("rbhqk,rbkhe->rbqhe", grad_scores, key_rows, preferred_element_type=jnp.float32)
        * HEAD_DIM ** (-0.5)
    ).astype(jnp.bfloat16)
    grad_keys = (
        jnp.einsum(
            "rbhqk,rbqhe->rbkhe", grad_scores, query_rows, preferred_element_type=jnp.float32
        )
        * HEAD_DIM ** (-0.5)
    ).astype(jnp.bfloat16)
    return (grad_query, grad_keys, grad_values)


def per_device(
    image_tokens,
    caption_embed,
    caption_lengths,
    output_grad,
    norm_self,
    norm_cross,
    norm_feed,
    self_query,
    self_key,
    self_value,
    self_output,
    cross_query,
    cross_key,
    cross_value,
    cross_output,
    up_weight,
    down_weight,
):
    gathered = (
        lax.all_gather(norm_self, "rows", axis=0, tiled=True),
        lax.all_gather(norm_cross, "rows", axis=0, tiled=True),
        lax.all_gather(norm_feed, "rows", axis=0, tiled=True),
        lax.all_gather(self_query, "rows", axis=0, tiled=True),
        lax.all_gather(self_key, "rows", axis=0, tiled=True),
        lax.all_gather(self_value, "rows", axis=0, tiled=True),
        lax.all_gather(self_output, "rows", axis=1, tiled=True),
        lax.all_gather(cross_query, "rows", axis=0, tiled=True),
        lax.all_gather(cross_key, "rows", axis=0, tiled=True),
        lax.all_gather(cross_value, "rows", axis=0, tiled=True),
        lax.all_gather(cross_output, "rows", axis=1, tiled=True),
        lax.all_gather(up_weight, "rows", axis=0, tiled=True),
        lax.all_gather(down_weight, "rows", axis=1, tiled=True),
    )
    gain_one = gathered[0].astype(jnp.float32)
    gain_two = gathered[1].astype(jnp.float32)
    gain_three = gathered[2].astype(jnp.float32)
    residual = image_tokens.astype(jnp.float32)
    normed_one, inverse_one = layer_stats(residual)
    first_input_tensor = gather_tokens((normed_one * gain_one).astype(jnp.bfloat16))
    query_one = split_heads(project(first_input_tensor, gathered[3]), IMAGE_TOKENS)
    key_one = split_heads(project(first_input_tensor, gathered[4]), IMAGE_TOKENS)
    value_one = split_heads(project(first_input_tensor, gathered[5]), IMAGE_TOKENS)
    mixed_one, logsum_one = attend_forward(query_one, key_one, value_one, None)
    merged_one = join_heads(mixed_one)
    residual_two = residual + sum_tokens(product(merged_one, gathered[6]))
    normed_two, inverse_two = layer_stats(residual_two)
    input_two = gather_tokens((normed_two * gain_two).astype(jnp.bfloat16))
    caption_full = lax.all_gather(caption_embed, "text", axis=1, tiled=True)
    query_two = split_heads(project(input_two, gathered[7]), IMAGE_TOKENS)
    key_two = split_heads(project(caption_full, gathered[8]), CAP)
    value_two = split_heads(project(caption_full, gathered[9]), CAP)
    slot_index = lax.broadcasted_iota(jnp.int32, (1, 1, CAP), 2)
    live_slots = (slot_index < caption_lengths[:, :, None])[:, :, None, None, :]
    mixed_two, logsum_two = attend_forward(query_two, key_two, value_two, live_slots)
    merged_two = join_heads(mixed_two)
    residual_three = residual_two + sum_tokens(product(merged_two, gathered[10]))
    normed_three, inverse_three = layer_stats(residual_three)
    input_three = gather_tokens((normed_three * gain_three).astype(jnp.bfloat16))
    hidden_pre = product(input_three, gathered[11])
    hidden_act = jax.nn.gelu(hidden_pre, approximate=False).astype(jnp.bfloat16)
    block_out = residual_three + sum_tokens(product(hidden_act, gathered[12]))
    grad_resid = output_grad.astype(jnp.float32)
    grad_full = gather_grads(grad_resid.astype(jnp.bfloat16))
    grad_down = contract_product(hidden_act, grad_full)
    grad_act = jnp.einsum(
        "rsd,fd->rsf", grad_full, gathered[12], preferred_element_type=jnp.float32
    )
    grad_pre = gelu_back(hidden_pre, grad_act).astype(jnp.bfloat16)
    grad_up = contract_product(input_three, grad_pre)
    grad_norm = sum_inputs(product_back(grad_pre, gathered[11]))
    grad_input, feed_gain_grad = norm_back(grad_norm, normed_three, inverse_three, gain_three)
    grad_resid = grad_resid + grad_input
    grad_full = gather_grads(grad_resid.astype(jnp.bfloat16))
    grad_cout = contract_product(merged_two, grad_full)
    grad_merged = jnp.einsum(
        "rsd,ed->rse", grad_full, gathered[10], preferred_element_type=jnp.float32
    ).astype(jnp.bfloat16)
    cross_gq, cross_gk, cross_gv = attend_back(
        query_two,
        key_two,
        value_two,
        live_slots,
        logsum_two,
        split_heads(grad_merged, IMAGE_TOKENS),
    )
    cross_gq = join_heads(cross_gq)
    cross_gk = join_heads(cross_gk)
    cross_gv = join_heads(cross_gv)
    grad_cquery = contract_product(input_two, cross_gq)
    grad_ckey = contract_product(caption_full, cross_gk)
    grad_cvalue = contract_product(caption_full, cross_gv)
    caption_grad = lax.psum_scatter(
        (product_back(cross_gk, gathered[8]) + product_back(cross_gv, gathered[9])).astype(
            jnp.bfloat16
        ),
        "text",
        scatter_dimension=1,
        tiled=True,
    ).astype(jnp.float32)
    grad_norm = sum_inputs(product_back(cross_gq, gathered[7]))
    grad_input, cross_gain_grad = norm_back(grad_norm, normed_two, inverse_two, gain_two)
    grad_resid = grad_resid + grad_input
    grad_full = gather_grads(grad_resid.astype(jnp.bfloat16))
    grad_sout = contract_product(merged_one, grad_full)
    grad_merged = jnp.einsum(
        "rsd,ed->rse", grad_full, gathered[6], preferred_element_type=jnp.float32
    ).astype(jnp.bfloat16)
    self_gq, self_key_gradient_part, self_gv = attend_back(
        query_one, key_one, value_one, None, logsum_one, split_heads(grad_merged, IMAGE_TOKENS)
    )
    self_gq = join_heads(self_gq)
    self_key_gradient_part = join_heads(self_key_gradient_part)
    self_gv = join_heads(self_gv)
    grad_squery = contract_product(first_input_tensor, self_gq)
    self_attention_key_gradient = contract_product(first_input_tensor, self_key_gradient_part)
    grad_svalue = contract_product(first_input_tensor, self_gv)
    grad_norm = sum_inputs(
        product_back(self_gq, gathered[3])
        + product_back(self_key_gradient_part, gathered[4])
        + product_back(self_gv, gathered[5])
    )
    grad_input, self_norm_gain_gradient = norm_back(grad_norm, normed_one, inverse_one, gain_one)
    grad_resid = grad_resid + grad_input
    gain_totals = lax.psum((self_norm_gain_gradient, cross_gain_grad, feed_gain_grad), "text")
    results = (
        lax.psum_scatter(
            gain_totals[0].astype(jnp.bfloat16), "rows", scatter_dimension=0, tiled=True
        ).astype(jnp.float32),
        lax.psum_scatter(
            gain_totals[1].astype(jnp.bfloat16), "rows", scatter_dimension=0, tiled=True
        ).astype(jnp.float32),
        lax.psum_scatter(
            gain_totals[2].astype(jnp.bfloat16), "rows", scatter_dimension=0, tiled=True
        ).astype(jnp.float32),
        lax.psum_scatter(
            grad_squery.astype(jnp.bfloat16), "rows", scatter_dimension=0, tiled=True
        ).astype(jnp.float32),
        lax.psum_scatter(
            self_attention_key_gradient.astype(jnp.bfloat16),
            "rows",
            scatter_dimension=0,
            tiled=True,
        ).astype(jnp.float32),
        lax.psum_scatter(
            grad_svalue.astype(jnp.bfloat16), "rows", scatter_dimension=0, tiled=True
        ).astype(jnp.float32),
        lax.psum_scatter(
            grad_sout.astype(jnp.bfloat16), "rows", scatter_dimension=1, tiled=True
        ).astype(jnp.float32),
        lax.psum_scatter(
            grad_cquery.astype(jnp.bfloat16), "rows", scatter_dimension=0, tiled=True
        ).astype(jnp.float32),
        lax.psum_scatter(
            grad_ckey.astype(jnp.bfloat16), "rows", scatter_dimension=0, tiled=True
        ).astype(jnp.float32),
        lax.psum_scatter(
            grad_cvalue.astype(jnp.bfloat16), "rows", scatter_dimension=0, tiled=True
        ).astype(jnp.float32),
        lax.psum_scatter(
            grad_cout.astype(jnp.bfloat16), "rows", scatter_dimension=1, tiled=True
        ).astype(jnp.float32),
        lax.psum_scatter(
            grad_up.astype(jnp.bfloat16), "rows", scatter_dimension=0, tiled=True
        ).astype(jnp.float32),
        lax.psum_scatter(
            grad_down.astype(jnp.bfloat16), "rows", scatter_dimension=1, tiled=True
        ).astype(jnp.float32),
    )
    return (
        block_out.astype(jnp.bfloat16),
        grad_resid,
        caption_grad,
        results[0],
        results[1],
        results[2],
        results[3],
        results[4],
        results[5],
        results[6],
        results[7],
        results[8],
        results[9],
        results[10],
        results[11],
        results[12],
    )


def solution(mesh):
    in_specs = (
        P("rows", "text", None),
        P("rows", "text", None),
        P("rows", None),
        P("rows", "text", None),
        P("rows"),
        P("rows"),
        P("rows"),
        P("rows", "text"),
        P("rows", "text"),
        P("rows", "text"),
        P("text", "rows"),
        P("rows", "text"),
        P("rows", "text"),
        P("rows", "text"),
        P("text", "rows"),
        P("rows", "text"),
        P("text", "rows"),
    )
    out_specs = (
        P("rows", "text", None),
        P("rows", "text", None),
        P("rows", "text", None),
        P("rows"),
        P("rows"),
        P("rows"),
        P("rows", "text"),
        P("rows", "text"),
        P("rows", "text"),
        P("text", "rows"),
        P("rows", "text"),
        P("rows", "text"),
        P("rows", "text"),
        P("text", "rows"),
        P("rows", "text"),
        P("text", "rows"),
    )
    return jax.shard_map(
        per_device, mesh=mesh, in_specs=in_specs, out_specs=out_specs, check_vma=False
    )
```

profile of v0, /device:TPU:0, one launch (start us, length us, event | category | flops | bytes accessed | tf_op | source)
XLA Modules:
  0.0 3408.7 jit_solution(11320915709437666502)
XLA Ops:
  14.3 185.2 %all-reduce.8 = (bf16[2048]{0:T(1024)(128)(2,1)S(1)}, bf16[2048]{0:T(1024)(128)(2,1)S(1)}, bf16[2048]{0:T(1024)(128)(2,1)}) all-reduce(bf16[2048]{0:T(1024)(128)(2,1)S(1)} %dynamic-update-slice, bf16[2048]{0:T(1024)(128)(2,1)S(1)} %dynamic-update-slice.1, ...), channel_id=1, replica_groups=mesh['rows'=32,'text'=4] {'rows'}, use_global_device_ids=true, to_apply=%add | all-reduce | flops 6144 | bytes 24576
  204.5 20.8 all-gather.17.cloned.1.call-done
  225.3 75.0 %all-gather.21.cloned.1.call-done = bf16[2048,512]{1,0:T(8,128)(2,1)} async-done(((bf16[64,512]{1,0:T(8,128)(2,1)}), bf16[2048,512]{1,0:T(8,128)(2,1)}) %all-gather.21.cloned.1.call-update) | async-done | bytes 2097168 | tf_op jit(solution)/shard_map/all_gather | solution.py:152
  300.3 3.5 fusion.56
  304.1 68.2 %all-gather.23.cloned.1.call-done = bf16[2048,512]{1,0:T(8,128)(2,1)} async-done(((bf16[64,512]{1,0:T(8,128)(2,1)}), bf16[2048,512]{1,0:T(8,128)(2,1)}) %all-gather.23.cloned.1.call-update) | async-done | bytes 2097168 | tf_op jit(solution)/shard_map/all_gather | solution.py:153
  372.4 3.5 fusion.59
  376.3 68.1 %all-gather.19.cloned.1.call-done = bf16[2048,512]{1,0:T(8,128)(2,1)} async-done(((bf16[64,512]{1,0:T(8,128)(2,1)}), bf16[2048,512]{1,0:T(8,128)(2,1)}) %all-gather.19.cloned.1.call-update) | async-done | bytes 2097168 | tf_op jit(solution)/shard_map/all_gather | solution.py:154
  444.3 3.5 fusion.53
  451.3 65.0 %all-gather.25.cloned.1.call-done = bf16[512,2048]{0,1:T(8,128)(2,1)} async-done(((bf16[512,64]{0,1:T(8,128)(2,1)}), bf16[512,2048]{0,1:T(8,128)(2,1)}) %all-gather.25.cloned.1.call-update) | async-done | bytes 2097168 | tf_op jit(solution)/shard_map/all_gather | solution.py:155
  516.3 4.9 convolution_bitcast_fusion.1
  523.5 41.4 %reduce-scatter.22.cloned.1.call-done = f32[1,128,2048]{2,1,0:T(8,128)} async-done(((f32[1,512,2048]{2,1,0:T(8,128)}), f32[1,128,2048]{2,1,0:T(8,128)}) %reduce-scatter.22.cloned.1.call-update) | async-done | bytes 1048592 | tf_op jit(solution)/shard_map/reduce_scatter | solution.py:40
  568.5 6.0 all_gather.66
  574.6 75.4 %all-gather.33.cloned.1.call-done = bf16[4096,512]{1,0:T(8,128)(2,1)} async-done(((bf16[128,512]{1,0:T(8,128)(2,1)}), bf16[4096,512]{1,0:T(8,128)(2,1)}) %all-gather.33.cloned.1.call-update) | async-done | bytes 4194320 | tf_op jit(solution)/shard_map/all_gather | solution.py:157
  650.0 3.0 convolution_convert_fusion.16
  653.6 79.3 %all-gather.27.cloned.1.call-done = bf16[4096,512]{1,0:T(8,128)(2,1)} async-done(((bf16[128,512]{1,0:T(8,128)(2,1)}), bf16[4096,512]{1,0:T(8,128)(2,1)}) %all-gather.27.cloned.1.call-update) | async-done | bytes 4194320 | tf_op jit(solution)/shard_map/all_gather | solution.py:158
  732.9 3.0 convolution_convert_fusion.17
  736.6 69.6 %all-gather.31.cloned.1.call-done = bf16[2048,512]{1,0:T(8,128)(2,1)} async-done(((bf16[64,512]{1,0:T(8,128)(2,1)}), bf16[2048,512]{1,0:T(8,128)(2,1)}) %all-gather.31.cloned.1.call-update) | async-done | bytes 2097168 | tf_op jit(solution)/shard_map/all_gather | solution.py:156
  806.1 29.3 all-gather.29.cloned.1.call-done
  835.5 4.3 fusion.62
  848.2 62.7 %all-gather.35.cloned.1.call-done = bf16[512,2048]{0,1:T(8,128)(2,1)} async-done(((bf16[512,64]{0,1:T(8,128)(2,1)}), bf16[512,2048]{0,1:T(8,128)(2,1)}) %all-gather.35.cloned.1.call-update) | async-done | bytes 2097168 | tf_op jit(solution)/shard_map/all_gather | solution.py:159
  910.9 5.1 convolution_bitcast_fusion
  917.5 42.2 %reduce-scatter.24.cloned.1.call-done = f32[1,128,2048]{2,1,0:T(8,128)} async-done(((f32[1,512,2048]{2,1,0:T(8,128)}), f32[1,128,2048]{2,1,0:T(8,128)}) %reduce-scatter.24.cloned.1.call-update) | async-done | bytes 1048592 | tf_op jit(solution)/shard_map/reduce_scatter | solution.py:40
  964.8 102.8 %all-gather.39.cloned.1.call-done = bf16[2048,2048]{1,0:T(8,128)(2,1)} async-done(((bf16[64,2048]{1,0:T(8,128)(2,1)}), bf16[2048,2048]{1,0:T(8,128)(2,1)}) %all-gather.39.cloned.1.call-update) | async-done | bytes 8388624 | tf_op jit(solution)/shard_map/all_gather | solution.py:160
  1067.7 29.0 all-gather.37.cloned.1.call-done
  1096.7 18.3 multiply_convert_fusion
  1115.0 13.2 all-gather.43.cloned.1.call-done
  1128.2 107.9 %all-gather.41.cloned.1.call-done = bf16[2048,2048]{0,1:T(8,128)(2,1)} async-done(((bf16[2048,64]{0,1:T(8,128)(2,1)}), bf16[2048,2048]{0,1:T(8,128)(2,1)}) %all-gather.41.cloned.1.call-update) | async-done | bytes 8388624 | tf_op jit(solution)/shard_map/all_gather | solution.py:161
  1236.1 12.0 add_convert_fusion.1
  1249.5 6.2 fusion.10
  1255.8 10.5 convolution_bitcast_fusion.2
  1266.4 15.6 reduce-scatter.28.cloned.1.call-done
  1285.0 45.8 %reduce-scatter.26.cloned.1.call-done = f32[1,128,2048]{2,1,0:T(8,128)} async-done(((f32[1,512,2048]{2,1,0:T(8,128)}), f32[1,128,2048]{2,1,0:T(8,128)}) %reduce-scatter.26.cloned.1.call-update) | async-done | bytes 1048592 | tf_op jit(solution)/shard_map/reduce_scatter | solution.py:40
  1330.7 3.9 fusion.171
  1335.5 29.3 all-gather.45.cloned.1.call-done
  1364.7 4.3 fusion.65
  1377.7 4.4 fusion.12
  1382.1 29.3 reduce-scatter.30.cloned.1.call-done
  1413.6 3.0 fusion.169
  1419.6 3.6 fusion.155
  1425.3 4.4 convolution_convert_fusion.4
  1429.8 4.2 convolution_convert_fusion.5
  1434.0 10.1 convolution_convert_fusion
  1444.4 10.0 convolution_convert_fusion.1
  1454.5 3.3 fusion.1
  1457.8 6.5 copy.121
  1465.1 3.3 fusion
  1468.4 6.6 copy.119
  1476.0 4.3 convolution_convert_fusion.6
  1480.6 3.5 fusion.68
  1491.0 4.4 convolution_convert_fusion.8
  1499.7 4.3 convolution_convert_fusion.9
  1506.8 3.0 fusion.107
  1519.2 139.2 %reduce-scatter.46.cloned.1.call-done = bf16[512,64]{0,1:T(8,128)(2,1)} async-done(((bf16[512,2048]{0,1:T(8,128)(2,1)}), bf16[512,64]{0,1:T(8,128)(2,1)}) %reduce-scatter.46.cloned.1.call-update) | async-done | bytes 65552 | tf_op jit(solution)/shard_map/reduce_scatter | solution.py:288
  1659.9 182.9 %reduce-scatter.44.cloned.1.call-done = bf16[64,512]{1,0:T(8,128)(2,1)} async-done(((bf16[2048,512]{1,0:T(8,128)(2,1)}), bf16[64,512]{1,0:T(8,128)(2,1)}) %reduce-scatter.44.cloned.1.call-update) | async-done | bytes 65552 | tf_op jit(solution)/shard_map/reduce_scatter | solution.py:279
  1844.3 198.5 %reduce-scatter.50.cloned.1.call-done = bf16[2048,64]{0,1:T(8,128)(2,1)} async-done(((bf16[2048,2048]{0,1:T(8,128)(2,1)}), bf16[2048,64]{0,1:T(8,128)(2,1)}) %reduce-scatter.50.cloned.1.call-update) | async-done | bytes 262160 | tf_op jit(solution)/shard_map/reduce_scatter | solution.py:294
  2044.6 198.3 %reduce-scatter.48.cloned.1.call-done = bf16[64,2048]{1,0:T(8,128)(2,1)} async-done(((bf16[2048,2048]{1,0:T(8,128)(2,1)}), bf16[64,2048]{1,0:T(8,128)(2,1)}) %reduce-scatter.48.cloned.1.call-update) | async-done | bytes 262160 | tf_op jit(solution)/shard_map/reduce_scatter | solution.py:291
  2244.7 187.7 %reduce-scatter.54.cloned.1.call-done = bf16[128,512]{1,0:T(8,128)(2,1)} async-done(((bf16[4096,512]{1,0:T(8,128)(2,1)}), bf16[128,512]{1,0:T(8,128)(2,1)}) %reduce-scatter.54.cloned.1.call-update) | async-done | bytes 131088
  2434.3 187.5 %reduce-scatter.52.cloned.1.call-done = bf16[128,512]{1,0:T(8,128)(2,1)} async-done(((bf16[4096,512]{1,0:T(8,128)(2,1)}), bf16[128,512]{1,0:T(8,128)(2,1)}) %reduce-scatter.52.cloned.1.call-update) | async-done | bytes 131088
  2623.7 182.4 %reduce-scatter.42.cloned.1.call-done = bf16[512,64]{0,1:T(8,128)(2,1)} async-done(((bf16[512,2048]{0,1:T(8,128)(2,1)}), bf16[512,64]{0,1:T(8,128)(2,1)}) %reduce-scatter.42.cloned.1.call-update) | async-done | bytes 65552 | tf_op jit(solution)/shard_map/reduce_scatter | solution.py:276
  2807.5 182.7 %reduce-scatter.38.cloned.1.call-done = bf16[64,512]{1,0:T(8,128)(2,1)} async-done(((bf16[2048,512]{1,0:T(8,128)(2,1)}), bf16[64,512]{1,0:T(8,128)(2,1)}) %reduce-scatter.38.cloned.1.call-update) | async-done | bytes 65552 | tf_op jit(solution)/shard_map/reduce_scatter | solution.py:267
  2991.7 182.8 %reduce-scatter.36.cloned.1.call-done = bf16[64,512]{1,0:T(8,128)(2,1)} async-done(((bf16[2048,512]{1,0:T(8,128)(2,1)}), bf16[64,512]{1,0:T(8,128)(2,1)}) %reduce-scatter.36.cloned.1.call-update) | async-done | bytes 65552 | tf_op jit(solution)/shard_map/reduce_scatter | solution.py:264
  3176.0 24.0 reduce-scatter.32.cloned.1.call-done
  3201.5 10.3 all-reduce.6
  3211.8 183.9 %all-reduce.7 = (bf16[2048]{0:T(1024)(128)(2,1)S(1)}, bf16[2048]{0:T(1024)(128)(2,1)S(1)}, bf16[2048]{0:T(1024)(128)(2,1)S(1)}) all-reduce(bf16[2048]{0:T(1024)(128)(2,1)S(1)} %get-tuple-element.73, bf16[2048]{0:T(1024)(128)(2,1)S(1)} %get-tuple-element.74, ...), channel_id=9, replica_groups=mesh['rows'=32,'text'=4] {'rows'}, use_global_device_ids=true, to_apply=%region_27.28.clone | all-reduce | flops 6144 | bytes 24576
  (255 shorter events, 105.8 us)
Async XLA Ops:
  7.2 218.1 %all-gather.17.cloned.1.call-start = ((), (), s32[]{:S(2)}) async-start(), calls=%async_computation.17 | async-start | bytes 2621440 | tf_op jit(solution)/shard_map/all_gather | solution.py:36
  8.4 216.9 %copy-start.36 = (f32[128]{0:T(128)}, f32[128]{0:T(128)S(1)}, u32[]{:S(2)}) copy-start(f32[128]{0:T(128)S(1)} %broadcast_multiply_fusion.8) | copy-start | bytes 1540
  9.8 215.5 %copy-start.40 = (f32[128]{0:T(128)}, f32[128]{0:T(128)S(1)}, u32[]{:S(2)}) copy-start(f32[128]{0:T(128)S(1)} %add_rsqrt_fusion.2) | copy-start | bytes 1540
  199.5 25.8 copy-start.23
  201.8 98.5 %all-gather.21.cloned.1.call-start = ((), (), s32[]{:S(2)}) async-start(), calls=%async_computation.19 | async-start | bytes 2162688 | tf_op jit(solution)/shard_map/all_gather | solution.py:152
  202.5 169.9 %all-gather.23.cloned.1.call-start = ((), (), s32[]{:S(2)}) async-start(), calls=%async_computation.20 | async-start | bytes 2162688 | tf_op jit(solution)/shard_map/all_gather | solution.py:153
  203.3 241.1 %all-gather.19.cloned.1.call-start = ((), (), s32[]{:S(2)}) async-start(), calls=%async_computation.18 | async-start | bytes 2162688 | tf_op jit(solution)/shard_map/all_gather | solution.py:154
  203.8 312.5 %all-gather.25.cloned.1.call-start = ((), (), s32[]{:S(2)}) async-start(), calls=%async_computation.21 | async-start | bytes 2162688 | tf_op jit(solution)/shard_map/all_gather | solution.py:155
  204.4 360.5 %reduce-scatter.22.cloned.1.call-start = ((), (), s32[]{:S(2)}) async-start(), calls=%async_computation.22 | async-start | bytes 5242880 | tf_op jit(solution)/shard_map/reduce_scatter | solution.py:40
  304.1 144.6 %copy-start.6 = (bf16[2,256,4,128]{1,3,2,0:T(8,128)(2,1)}, bf16[2,256,4,128]{1,3,2,0:T(8,128)(2,1)S(1)}, u32[]{:S(2)}) copy-start(bf16[2,256,4,128]{1,3,2,0:T(8,128)(2,1)S(1)} %copy.103) | copy-start | bytes 1572868
  376.3 72.5 %copy-start.5 = (bf16[2,256,4,128]{1,3,2,0:T(8,128)(2,1)}, bf16[2,256,4,128]{1,3,2,0:T(8,128)(2,1)S(1)}, u32[]{:S(2)}) copy-start(bf16[2,256,4,128]{1,3,2,0:T(8,128)(2,1)S(1)} %copy.100) | copy-start | bytes 1572868
  451.3 69.8 %copy-start.17 = (bf16[1,2,256,4,128]{4,3,2,1,0:T(4,128)(2,1)}, bf16[1,2,256,4,128]{4,3,2,1,0:T(4,128)(2,1)S(1)}, u32[]{:S(2)}) copy-start(bf16[1,2,256,4,128]{4,3,2,1,0:T(4,128)(2,1)S(1)} %copy.89) | copy-start | bytes 1572868
  521.2 47.4 %copy-start.29 = (bf16[1,8,4096]{2,1,0:T(8,128)(2,1)S(1)}, bf16[1,8,4096]{2,1,0:T(8,128)(2,1)}, u32[]{:S(2)}) copy-start(bf16[1,8,4096]{2,1,0:T(8,128)(2,1)} %param.18) | copy-start | bytes 196612
  521.2 53.3 %copy-start.45 = (s32[1,2]{1,0:T(1,128)S(1)}, s32[1,2]{1,0:T(1,128)}, u32[]{:S(2)}) copy-start(s32[1,2]{1,0:T(1,128)} %param.19) | copy-start | bytes 28
  521.2 128.8 %all-gather.33.cloned.1.call-start = ((), (), s32[]{:S(2)}) async-start(), calls=%async_computation.26 | async-start | bytes 4325376 | tf_op jit(solution)/shard_map/all_gather | solution.py:157
  522.0 211.0 %all-gather.27.cloned.1.call-start = ((), (), s32[]{:S(2)}) async-start(), calls=%async_computation.23 | async-start | bytes 4325376 | tf_op jit(solution)/shard_map/all_gather | solution.py:158
  522.7 283.4 %all-gather.31.cloned.1.call-start = ((), (), s32[]{:S(2)}) async-start(), calls=%async_computation.25 | async-start | bytes 2162688 | tf_op jit(solution)/shard_map/all_gather | solution.py:156
  523.4 312.0 %all-gather.29.cloned.1.call-start = ((), (), s32[]{:S(2)}) async-start(), calls=%async_computation.24 | async-start | bytes 2621440 | tf_op jit(solution)/shard_map/all_gather | solution.py:36
  566.4 169.5 %copy-start.38 = (f32[128]{0:T(128)}, f32[128]{0:T(128)S(1)}, u32[]{:S(2)}) copy-start(f32[128]{0:T(128)S(1)} %broadcast_multiply_fusion.7) | copy-start | bytes 1540
  566.7 169.2 %copy-start.42 = (f32[128]{0:T(128)}, f32[128]{0:T(128)S(1)}, u32[]{:S(2)}) copy-start(f32[128]{0:T(128)S(1)} %add_rsqrt_fusion.1) | copy-start | bytes 1540
  567.7 343.2 %all-gather.35.cloned.1.call-start = ((), (), s32[]{:S(2)}) async-start(), calls=%async_computation.27 | async-start | bytes 2162688 | tf_op jit(solution)/shard_map/all_gather | solution.py:159
  568.5 391.2 %reduce-scatter.24.cloned.1.call-start = ((), (), s32[]{:S(2)}) async-start(), calls=%async_computation.28 | async-start | bytes 5242880 | tf_op jit(solution)/shard_map/reduce_scatter | solution.py:40
  574.6 268.5 %copy-start.35 = (pred[2,16]{1,0:T(4,128)(4,1)}, pred[2,16]{1,0:T(4,128)(4,1)S(1)}, u32[]{:S(2)}) copy-start(pred[2,16]{1,0:T(4,128)(4,1)S(1)} %iota_compare_fusion) | copy-start | bytes 100
  916.0 151.7 %all-gather.39.cloned.1.call-start = ((), (), s32[]{:S(2)}) async-start(), calls=%async_computation.30 | async-start | bytes 8650752 | tf_op jit(solution)/shard_map/all_gather | solution.py:160
  916.8 179.9 %all-gather.37.cloned.1.call-start = ((), (), s32[]{:S(2)}) async-start(), calls=%async_computation.29 | async-start | bytes 2621440 | tf_op jit(solution)/shard_map/all_gather | solution.py:36
  963.6 164.5 %all-gather.43.cloned.1.call-start = ((), (), s32[]{:S(2)}) async-start(), calls=%async_computation.33 | async-start | bytes 2621440 | tf_op jit(solution)/shard_map/all_gather | solution.py:44
  964.2 271.9 %all-gather.41.cloned.1.call-start = ((), (), s32[]{:S(2)}) async-start(), calls=%async_computation.31 | async-start | bytes 8650752 | tf_op jit(solution)/shard_map/all_gather | solution.py:161
  964.8 317.2 %reduce-scatter.28.cloned.1.call-start = ((), (), s32[]{:S(2)}) async-start(), calls=%async_computation.34 | async-start | bytes 2621440 | tf_op jit(solution)/shard_map/reduce_scatter | solution.py:48
  1236.1 13.4 copy-start.43
  1255.7 75.0 %reduce-scatter.26.cloned.1.call-start = ((), (), s32[]{:S(2)}) async-start(), calls=%async_computation.32 | async-start | bytes 5242880 | tf_op jit(solution)/shard_map/reduce_scatter | solution.py:40
  1266.3 98.4 %all-gather.45.cloned.1.call-start = ((), (), s32[]{:S(2)}) async-start(), calls=%async_computation.35 | async-start | bytes 2621440 | tf_op jit(solution)/shard_map/all_gather | solution.py:44
  1334.7 76.8 %reduce-scatter.30.cloned.1.call-start = ((), (), s32[]{:S(2)}) async-start(), calls=%async_computation.36 | async-start | bytes 2621440 | tf_op jit(solution)/shard_map/reduce_scatter | solution.py:48
  1382.1 93.0 %all-gather.47.cloned.1.call-start = ((), (), s32[]{:S(2)}) async-start(), calls=%async_computation.37 | async-start | bytes 2621440 | tf_op jit(solution)/shard_map/all_gather | solution.py:44
  1416.6 101.1 %reduce-scatter.34.cloned.1.call-start = ((), (), s32[]{:S(2)}) async-start(), calls=%async_computation.39 | async-start | bytes 327680 | tf_op jit(solution)/shard_map/reduce_scatter | solution.py:221
  1416.8 6.4 copy-start.2
  1418.2 4.9 copy-start.21
  1419.6 5.7 copy-start.19
  1425.2 4.5 copy-start.20
  1425.2 233.2 %reduce-scatter.46.cloned.1.call-start = ((), (), s32[]{:S(2)}) async-start(), calls=%async_computation.45 | async-start | bytes 2162688 | tf_op jit(solution)/shard_map/reduce_scatter | solution.py:288
  1429.7 413.1 %reduce-scatter.44.cloned.1.call-start = ((), (), s32[]{:S(2)}) async-start(), calls=%async_computation.44 | async-start | bytes 2162688 | tf_op jit(solution)/shard_map/reduce_scatter | solution.py:279
  1434.0 608.9 %reduce-scatter.50.cloned.1.call-start = ((), (), s32[]{:S(2)}) async-start(), calls=%async_computation.47 | async-start | bytes 8650752 | tf_op jit(solution)/shard_map/reduce_scatter | solution.py:294
  1444.2 798.8 %reduce-scatter.48.cloned.1.call-start = ((), (), s32[]{:S(2)}) async-start(), calls=%async_computation.46 | async-start | bytes 8650752 | tf_op jit(solution)/shard_map/reduce_scatter | solution.py:291
  1454.5 978.0 %reduce-scatter.54.cloned.1.call-start = ((), (), s32[]{:S(2)}) async-start(), calls=%async_computation.49 | async-start | bytes 4325376
  1464.4 1157.5 %reduce-scatter.52.cloned.1.call-start = ((), (), s32[]{:S(2)}) async-start(), calls=%async_computation.48 | async-start | bytes 4325376
  1475.0 5.6 copy-start.26
  1475.0 5.6 copy-start.31
  1475.0 1331.0 %reduce-scatter.42.cloned.1.call-start = ((), (), s32[]{:S(2)}) async-start(), calls=%async_computation.43 | async-start | bytes 2162688 | tf_op jit(solution)/shard_map/reduce_scatter | solution.py:276
  1480.3 1509.9 %reduce-scatter.38.cloned.1.call-start = ((), (), s32[]{:S(2)}) async-start(), calls=%async_computation.41 | async-start | bytes 2162688 | tf_op jit(solution)/shard_map/reduce_scatter | solution.py:267
  1480.6 5.7 copy-start.14
  1495.4 1679.1 %reduce-scatter.36.cloned.1.call-start = ((), (), s32[]{:S(2)}) async-start(), calls=%async_computation.40 | async-start | bytes 2162688 | tf_op jit(solution)/shard_map/reduce_scatter | solution.py:264
  1499.7 4.4 copy-start.4
  1504.0 2.8 copy-start.9
  1504.1 1695.9 %reduce-scatter.32.cloned.1.call-start = ((), (), s32[]{:S(2)}) async-start(), calls=%async_computation.38 | async-start | bytes 2621440 | tf_op jit(solution)/shard_map/reduce_scatter | solution.py:48
  1506.8 3.1 copy-start.11
  1506.8 3.1 copy-start.15
  1511.5 2.7 copy-start.44
  1514.1 1883.3 %reduce-scatter.40.cloned.1.call-start = ((), (), s32[]{:S(2)}) async-start(), calls=%async_computation.42 | async-start | bytes 2162688 | tf_op jit(solution)/shard_map/reduce_scatter | solution.py:273
  1516.8 1683.2 %copy-start.1 = (bf16[1,128,2048]{2,1,0:T(8,128)(2,1)S(1)}, bf16[1,128,2048]{2,1,0:T(8,128)(2,1)}, u32[]{:S(2)}) copy-start(bf16[1,128,2048]{2,1,0:T(8,128)(2,1)} %param.17) | copy-start | bytes 1572868
  1516.8 1683.2 %copy-start.24 = (f32[2048]{0:T(1024)S(1)}, f32[2048]{0:T(1024)}, u32[]{:S(2)}) copy-start(f32[2048]{0:T(1024)} %copy-done.23) | copy-start | bytes 24580
  1516.8 1683.2 %copy-start.37 = (f32[128]{0:T(128)S(1)}, f32[128]{0:T(128)}, u32[]{:S(2)}) copy-start(f32[128]{0:T(128)} %copy-done.36) | copy-start | bytes 1540
  1516.8 1683.2 %copy-start.41 = (f32[128]{0:T(128)S(1)}, f32[128]{0:T(128)}, u32[]{:S(2)}) copy-start(f32[128]{0:T(128)} %copy-done.40) | copy-start | bytes 1540
  1516.8 1684.7 %copy-start.32 = (f32[2048]{0:T(1024)S(1)}, f32[2048]{0:T(1024)}, u32[]{:S(2)}) copy-start(f32[2048]{0:T(1024)} %get-tuple-element.64) | copy-start | bytes 24580
  1516.8 1684.7 %copy-start.33 = (f32[2048]{0:T(1024)S(1)}, f32[2048]{0:T(1024)}, u32[]{:S(2)}) copy-start(f32[2048]{0:T(1024)} %get-tuple-element.66) | copy-start | bytes 24580
  1516.9 1882.1 %copy-start.8 = (f32[1,128,2048]{2,1,0:T(8,128)S(1)}, f32[1,128,2048]{2,1,0:T(8,128)}, u32[]{:S(2)}) copy-start(f32[1,128,2048]{2,1,0:T(8,128)} %get-tuple-element.83) | copy-start | bytes 3145732
  (16 other events, 14.8 us)
Sparse Core Ops, SparseCore 0:
  201.9 23.3 all-gather.16
  228.5 71.7 all-gather.20
  303.4 68.9 all-gather.22
  375.4 68.9 all-gather.18
  447.4 68.9 all-gather.24
  521.3 43.5 reduce-scatter.21
  568.5 81.4 all-gather.32
  653.6 79.2 all-gather.26
  736.6 69.5 all-gather.30
  808.3 27.1 all-gather.28
  839.1 71.7 all-gather.34
  916.1 43.5 reduce-scatter.23
  962.9 104.7 all-gather.38
  1069.8 26.8 all-gather.36
  1098.2 29.9 all-gather.42
  1131.2 104.8 all-gather.40
  1255.9 26.1 reduce-scatter.27
  1284.4 46.2 reduce-scatter.25
  1334.8 29.8 all-gather.44
  1382.2 29.2 reduce-scatter.29
  1416.7 29.8 all-gather.46
  1449.7 18.2 reduce-scatter.33
  1470.4 188.0 reduce-scatter.45
  1660.8 182.0 reduce-scatter.43
  1845.2 197.5 reduce-scatter.49
  2045.1 197.7 reduce-scatter.47
  2245.2 187.2 reduce-scatter.53
  2434.8 186.9 reduce-scatter.51
  2624.2 181.7 reduce-scatter.41
  2808.4 181.7 reduce-scatter.37
  2992.6 181.8 reduce-scatter.35
  3177.1 22.8 reduce-scatter.31
  3202.2 188.5 reduce-scatter.39
where the time goes:
time: 3420 us; the launch traced here: 3410 us
  waiting for transfers between devices  2740 us (80%)
  blocking collectives  385 us (11%)
  matrix products  169 us (5%)
  local copies, waits for them, and re-layouts  47 us (1%)
  other arithmetic  45.3 us (1%)
    unnamed x35, waiting for transfers between devices  383 us
    unnamed x2, blocking collectives  369 us
    reduce_scatter x1, waiting for transfers between devices, per_device(): lax.psum_scatter(grad_down.astype(jnp.bfloat16), 'rows', scatter_dimensio...  199 us
    reduce_scatter x1, waiting for transfers between devices, per_device(): lax.psum_scatter(grad_up.astype(jnp.bfloat16), 'rows', scatter_dimension=...  198 us
    reduce_scatter x1, waiting for transfers between devices, per_device(): lax.psum_scatter(grad_cquery.astype(jnp.bfloat16), 'rows', scatter_dimens...  183 us
    reduce_scatter x1, waiting for transfers between devices, per_device(): lax.psum_scatter(grad_squery.astype(jnp.bfloat16), 'rows', scatter_dimens...  183 us
    reduce_scatter x1, waiting for transfers between devices, per_device(): lax.psum_scatter(self_attention_key_gradient.astype(jnp.bfloat16), 'rows'...  183 us
    reduce_scatter x1, waiting for transfers between devices, per_device(): lax.psum_scatter(grad_sout.astype(jnp.bfloat16), 'rows', scatter_dimensio...  182 us
  transfers between devices with their start and end apart: 33, of which 30 were waited for; matrix products, arithmetic and copies ran while one was open for 5% of the time, Pallas kernels for 0%

commit v1 on v0

--- a/solution.py
+++ b/solution.py
@@ -154,7 +154,9 @@
         lax.all_gather(self_value, "rows", axis=0, tiled=True),
         lax.all_gather(self_output, "rows", axis=1, tiled=True),
         lax.all_gather(cross_query, "rows", axis=0, tiled=True),
-        lax.all_gather(cross_key, "rows", axis=0, tiled=True),
+        jnp.concatenate(
+            lax.all_to_all(jnp.stack([cross_key] * lax.axis_size("rows")), "rows", 0, 0), axis=0
+        ),
         lax.all_gather(cross_value, "rows", axis=0, tiled=True),
         lax.all_gather(cross_output, "rows", axis=1, tiled=True),
         lax.all_gather(up_weight, "rows", axis=0, tiled=True),

time: 3420 us -> 3380 us (0.988)
  waiting for transfers between devices: 2740 us -> 2640 us
  blocking collectives: 385 us -> 434 us
    all_gather x1 -> x0, waiting for transfers between devices: 75.4 us -> none  [per_device(): lax.all_gather(cross_key, 'rows', axis=0, tiled=True)]
    all_gather x1, blocking collectives: 6 us -> 54.8 us  [per_device(): caption_full = lax.all_gather(caption_embed, 'text', axis=1, tiled=True)]
    unnamed x35 -> x34, waiting for transfers between devices: 383 us -> 382 us
  transfers between devices with their start and end apart: 33 -> 33, of which waited for: 30 -> 29; matrix products, arithmetic and copies ran while one was open for 5% -> 6% of each run, Pallas kernels for 0% -> 0%
where the time goes in v1:
time: 3380 us; the launch traced here: 3370 us
  waiting for transfers between devices  2640 us (78%)
  blocking collectives  434 us (13%)
  matrix products  169 us (5%)
  local copies, waits for them, and re-layouts  49.5 us (1%)
  other arithmetic  45.2 us (1%)
    unnamed x34, waiting for transfers between devices  382 us
    unnamed x2, blocking collectives  369 us
    reduce_scatter x1, waiting for transfers between devices, per_device(): lax.psum_scatter(grad_down.astype(jnp.bfloat16), 'rows', scatter_dimensio...  199 us
    reduce_scatter x1, waiting for transfers between devices, per_device(): lax.psum_scatter(grad_up.astype(jnp.bfloat16), 'rows', scatter_dimension=...  198 us
    reduce_scatter x1, waiting for transfers between devices, per_device(): lax.psum_scatter(self_attention_key_gradient.astype(jnp.bfloat16), 'rows'...  183 us
    reduce_scatter x1, waiting for transfers between devices, per_device(): lax.psum_scatter(grad_cquery.astype(jnp.bfloat16), 'rows', scatter_dimens...  183 us
    reduce_scatter x1, waiting for transfers between devices, per_device(): lax.psum_scatter(grad_sout.astype(jnp.bfloat16), 'rows', scatter_dimensio...  183 us
    reduce_scatter x1, waiting for transfers between devices, per_device(): lax.psum_scatter(grad_squery.astype(jnp.bfloat16), 'rows', scatter_dimens...  183 us
  transfers between devices with their start and end apart: 33, of which 29 were waited for; matrix products, arithmetic and copies ran while one was open for 6% of the time, Pallas kernels for 0%

profile of v1, /device:TPU:0, one launch (start us, length us, event | category | flops | bytes accessed | tf_op | source)
XLA Modules:
  0.0 3368.5 jit_solution(4046444457297018939)
XLA Ops:
  14.3 185.2 %all-reduce.8 = (bf16[2048]{0:T(1024)(128)(2,1)S(1)}, bf16[2048]{0:T(1024)(128)(2,1)S(1)}, bf16[2048]{0:T(1024)(128)(2,1)}) all-reduce(bf16[2048]{0:T(1024)(128)(2,1)S(1)} %dynamic-update-slice, bf16[2048]{0:T(1024)(128)(2,1)S(1)} %dynamic-update-slice.1, ...), channel_id=1, replica_groups=mesh['rows'=32,'text'=4] {'rows'}, use_global_device_ids=true, to_apply=%add | all-reduce | flops 6144 | bytes 24576
  204.5 20.8 all-gather.16.cloned.1.call-done
  225.3 75.0 %all-gather.20.cloned.1.call-done = bf16[2048,512]{1,0:T(8,128)(2,1)} async-done(((bf16[64,512]{1,0:T(8,128)(2,1)}), bf16[2048,512]{1,0:T(8,128)(2,1)}) %all-gather.20.cloned.1.call-update) | async-done | bytes 2097168 | tf_op jit(solution)/shard_map/all_gather | solution.py:152
  300.3 3.5 fusion.56
  304.1 68.2 %all-gather.22.cloned.1.call-done = bf16[2048,512]{1,0:T(8,128)(2,1)} async-done(((bf16[64,512]{1,0:T(8,128)(2,1)}), bf16[2048,512]{1,0:T(8,128)(2,1)}) %all-gather.22.cloned.1.call-update) | async-done | bytes 2097168 | tf_op jit(solution)/shard_map/all_gather | solution.py:153
  372.4 3.5 fusion.59
  376.3 68.1 %all-gather.18.cloned.1.call-done = bf16[2048,512]{1,0:T(8,128)(2,1)} async-done(((bf16[64,512]{1,0:T(8,128)(2,1)}), bf16[2048,512]{1,0:T(8,128)(2,1)}) %all-gather.18.cloned.1.call-update) | async-done | bytes 2097168 | tf_op jit(solution)/shard_map/all_gather | solution.py:154
  444.3 3.5 fusion.53
  451.3 65.0 %all-gather.24.cloned.1.call-done = bf16[512,2048]{0,1:T(8,128)(2,1)} async-done(((bf16[512,64]{0,1:T(8,128)(2,1)}), bf16[512,2048]{0,1:T(8,128)(2,1)}) %all-gather.24.cloned.1.call-update) | async-done | bytes 2097168 | tf_op jit(solution)/shard_map/all_gather | solution.py:155
  516.3 4.9 convolution_bitcast_fusion.1
  522.8 42.1 %reduce-scatter.22.cloned.1.call-done = f32[1,128,2048]{2,1,0:T(8,128)} async-done(((f32[1,512,2048]{2,1,0:T(8,128)}), f32[1,128,2048]{2,1,0:T(8,128)}) %reduce-scatter.22.cloned.1.call-update) | async-done | bytes 1048592 | tf_op jit(solution)/shard_map/reduce_scatter | solution.py:40
  570.2 9.7 all-to-all-start
  580.5 54.8 %all_gather.63 = bf16[1,32,4096]{2,1,0:T(8,128)(2,1)S(1)} all-gather(bf16[1,8,4096]{2,1,0:T(8,128)(2,1)S(1)} %copy-done.30), channel_id=1, replica_groups=mesh['rows'=32,'text'=4] {'text'}, dimensions={1}, use_global_device_ids=true | all-gather | bytes 327680 | tf_op jit(solution)/shard_map/all_gather | solution.py:179
  635.5 3.0 convolution_convert_fusion.16
  639.1 52.5 %all-gather.26.cloned.1.call-done = bf16[4096,512]{1,0:T(8,128)(2,1)} async-done(((bf16[128,512]{1,0:T(8,128)(2,1)}), bf16[4096,512]{1,0:T(8,128)(2,1)}) %all-gather.26.cloned.1.call-update) | async-done | bytes 4194320 | tf_op jit(solution)/shard_map/all_gather | solution.py:160
  691.6 3.0 convolution_convert_fusion.17
  695.2 69.6 %all-gather.30.cloned.1.call-done = bf16[2048,512]{1,0:T(8,128)(2,1)} async-done(((bf16[64,512]{1,0:T(8,128)(2,1)}), bf16[2048,512]{1,0:T(8,128)(2,1)}) %all-gather.30.cloned.1.call-update) | async-done | bytes 2097168 | tf_op jit(solution)/shard_map/all_gather | solution.py:156
  764.8 29.5 all-gather.28.cloned.1.call-done
  794.3 4.3 fusion.62
  807.1 62.5 %all-gather.32.cloned.1.call-done = bf16[512,2048]{0,1:T(8,128)(2,1)} async-done(((bf16[512,64]{0,1:T(8,128)(2,1)}), bf16[512,2048]{0,1:T(8,128)(2,1)}) %all-gather.32.cloned.1.call-update) | async-done | bytes 2097168 | tf_op jit(solution)/shard_map/all_gather | solution.py:161
  869.6 5.1 convolution_bitcast_fusion
  876.0 42.4 %reduce-scatter.24.cloned.1.call-done = f32[1,128,2048]{2,1,0:T(8,128)} async-done(((f32[1,512,2048]{2,1,0:T(8,128)}), f32[1,128,2048]{2,1,0:T(8,128)}) %reduce-scatter.24.cloned.1.call-update) | async-done | bytes 1048592 | tf_op jit(solution)/shard_map/reduce_scatter | solution.py:40
  923.5 102.7 %all-gather.36.cloned.1.call-done = bf16[2048,2048]{1,0:T(8,128)(2,1)} async-done(((bf16[64,2048]{1,0:T(8,128)(2,1)}), bf16[2048,2048]{1,0:T(8,128)(2,1)}) %all-gather.36.cloned.1.call-update) | async-done | bytes 8388624 | tf_op jit(solution)/shard_map/all_gather | solution.py:162
  1026.2 29.1 all-gather.34.cloned.1.call-done
  1055.3 18.3 multiply_convert_fusion
  1073.7 13.2 all-gather.40.cloned.1.call-done
  1086.8 107.9 %all-gather.38.cloned.1.call-done = bf16[2048,2048]{0,1:T(8,128)(2,1)} async-done(((bf16[2048,64]{0,1:T(8,128)(2,1)}), bf16[2048,2048]{0,1:T(8,128)(2,1)}) %all-gather.38.cloned.1.call-update) | async-done | bytes 8388624 | tf_op jit(solution)/shard_map/all_gather | solution.py:163
  1194.8 12.0 add_convert_fusion.1
  1208.2 6.2 fusion.10
  1214.5 10.5 convolution_bitcast_fusion.2
  1225.1 15.6 reduce-scatter.28.cloned.1.call-done
  1243.6 45.8 %reduce-scatter.26.cloned.1.call-done = f32[1,128,2048]{2,1,0:T(8,128)} async-done(((f32[1,512,2048]{2,1,0:T(8,128)}), f32[1,128,2048]{2,1,0:T(8,128)}) %reduce-scatter.26.cloned.1.call-update) | async-done | bytes 1048592 | tf_op jit(solution)/shard_map/reduce_scatter | solution.py:40
  1289.4 3.9 fusion.171
  1294.1 29.3 all-gather.42.cloned.1.call-done
  1323.4 4.3 fusion.65
  1336.2 4.4 fusion.12
  1340.7 29.3 reduce-scatter.30.cloned.1.call-done
  1372.1 3.0 fusion.169
  1378.1 3.6 fusion.155
  1383.8 4.4 convolution_convert_fusion.4
  1388.3 4.2 convolution_convert_fusion.5
  1392.6 10.1 convolution_convert_fusion
  1403.0 10.0 convolution_convert_fusion.1
  1413.1 3.3 fusion.1
  1416.4 6.5 copy.121
  1423.7 3.3 fusion
  1427.0 6.6 copy.119
  1434.6 4.3 convolution_convert_fusion.6
  1439.2 3.5 fusion.68
  1449.6 4.4 convolution_convert_fusion.8
  1458.3 4.3 convolution_convert_fusion.9
  1465.4 3.0 fusion.107
  1477.7 139.2 %reduce-scatter.46.cloned.1.call-done = bf16[512,64]{0,1:T(8,128)(2,1)} async-done(((bf16[512,2048]{0,1:T(8,128)(2,1)}), bf16[512,64]{0,1:T(8,128)(2,1)}) %reduce-scatter.46.cloned.1.call-update) | async-done | bytes 65552 | tf_op jit(solution)/shard_map/reduce_scatter | solution.py:290
  1618.5 183.0 %reduce-scatter.44.cloned.1.call-done = bf16[64,512]{1,0:T(8,128)(2,1)} async-done(((bf16[2048,512]{1,0:T(8,128)(2,1)}), bf16[64,512]{1,0:T(8,128)(2,1)}) %reduce-scatter.44.cloned.1.call-update) | async-done | bytes 65552 | tf_op jit(solution)/shard_map/reduce_scatter | solution.py:281
  1803.0 199.0 %reduce-scatter.50.cloned.1.call-done = bf16[2048,64]{0,1:T(8,128)(2,1)} async-done(((bf16[2048,2048]{0,1:T(8,128)(2,1)}), bf16[2048,64]{0,1:T(8,128)(2,1)}) %reduce-scatter.50.cloned.1.call-update) | async-done | bytes 262160 | tf_op jit(solution)/shard_map/reduce_scatter | solution.py:296
  2003.7 198.2 %reduce-scatter.48.cloned.1.call-done = bf16[64,2048]{1,0:T(8,128)(2,1)} async-done(((bf16[2048,2048]{1,0:T(8,128)(2,1)}), bf16[64,2048]{1,0:T(8,128)(2,1)}) %reduce-scatter.48.cloned.1.call-update) | async-done | bytes 262160 | tf_op jit(solution)/shard_map/reduce_scatter | solution.py:293
  2203.7 188.1 %reduce-scatter.54.cloned.1.call-done = bf16[128,512]{1,0:T(8,128)(2,1)} async-done(((bf16[4096,512]{1,0:T(8,128)(2,1)}), bf16[128,512]{1,0:T(8,128)(2,1)}) %reduce-scatter.54.cloned.1.call-update) | async-done | bytes 131088
  2393.6 187.7 %reduce-scatter.52.cloned.1.call-done = bf16[128,512]{1,0:T(8,128)(2,1)} async-done(((bf16[4096,512]{1,0:T(8,128)(2,1)}), bf16[128,512]{1,0:T(8,128)(2,1)}) %reduce-scatter.52.cloned.1.call-update) | async-done | bytes 131088
  2583.1 182.7 %reduce-scatter.42.cloned.1.call-done = bf16[512,64]{0,1:T(8,128)(2,1)} async-done(((bf16[512,2048]{0,1:T(8,128)(2,1)}), bf16[512,64]{0,1:T(8,128)(2,1)}) %reduce-scatter.42.cloned.1.call-update) | async-done | bytes 65552 | tf_op jit(solution)/shard_map/reduce_scatter | solution.py:278
  2767.4 183.1 %reduce-scatter.38.cloned.1.call-done = bf16[64,512]{1,0:T(8,128)(2,1)} async-done(((bf16[2048,512]{1,0:T(8,128)(2,1)}), bf16[64,512]{1,0:T(8,128)(2,1)}) %reduce-scatter.38.cloned.1.call-update) | async-done | bytes 65552 | tf_op jit(solution)/shard_map/reduce_scatter | solution.py:269
  2952.0 182.6 %reduce-scatter.36.cloned.1.call-done = bf16[64,512]{1,0:T(8,128)(2,1)} async-done(((bf16[2048,512]{1,0:T(8,128)(2,1)}), bf16[64,512]{1,0:T(8,128)(2,1)}) %reduce-scatter.36.cloned.1.call-update) | async-done | bytes 65552 | tf_op jit(solution)/shard_map/reduce_scatter | solution.py:266
  3136.1 24.0 reduce-scatter.32.cloned.1.call-done
  3161.6 10.3 all-reduce.6
  3171.9 183.9 %all-reduce.7 = (bf16[2048]{0:T(1024)(128)(2,1)S(1)}, bf16[2048]{0:T(1024)(128)(2,1)S(1)}, bf16[2048]{0:T(1024)(128)(2,1)S(1)}) all-reduce(bf16[2048]{0:T(1024)(128)(2,1)S(1)} %get-tuple-element.73, bf16[2048]{0:T(1024)(128)(2,1)S(1)} %get-tuple-element.74, ...), channel_id=9, replica_groups=mesh['rows'=32,'text'=4] {'rows'}, use_global_device_ids=true, to_apply=%region_27.28.clone | all-reduce | flops 6144 | bytes 24576
  (257 shorter events, 107.1 us)
Async XLA Ops:
  7.2 218.1 %all-gather.16.cloned.1.call-start = ((), (), s32[]{:S(2)}) async-start(), calls=%async_computation.18 | async-start | bytes 2621440 | tf_op jit(solution)/shard_map/all_gather | solution.py:36
  8.4 216.9 %copy-start.37 = (f32[128]{0:T(128)}, f32[128]{0:T(128)S(1)}, u32[]{:S(2)}) copy-start(f32[128]{0:T(128)S(1)} %broadcast_multiply_fusion.8) | copy-start | bytes 1540
  9.8 215.5 %copy-start.41 = (f32[128]{0:T(128)}, f32[128]{0:T(128)S(1)}, u32[]{:S(2)}) copy-start(f32[128]{0:T(128)S(1)} %add_rsqrt_fusion.2) | copy-start | bytes 1540
  199.5 25.8 copy-start.23
  201.8 98.5 %all-gather.20.cloned.1.call-start = ((), (), s32[]{:S(2)}) async-start(), calls=%async_computation.20 | async-start | bytes 2162688 | tf_op jit(solution)/shard_map/all_gather | solution.py:152
  202.5 169.9 %all-gather.22.cloned.1.call-start = ((), (), s32[]{:S(2)}) async-start(), calls=%async_computation.21 | async-start | bytes 2162688 | tf_op jit(solution)/shard_map/all_gather | solution.py:153
  203.3 241.1 %all-gather.18.cloned.1.call-start = ((), (), s32[]{:S(2)}) async-start(), calls=%async_computation.19 | async-start | bytes 2162688 | tf_op jit(solution)/shard_map/all_gather | solution.py:154
  203.8 312.5 %all-gather.24.cloned.1.call-start = ((), (), s32[]{:S(2)}) async-start(), calls=%async_computation.22 | async-start | bytes 2162688 | tf_op jit(solution)/shard_map/all_gather | solution.py:155
  204.4 360.5 %reduce-scatter.22.cloned.1.call-start = ((), (), s32[]{:S(2)}) async-start(), calls=%async_computation.23 | async-start | bytes 5242880 | tf_op jit(solution)/shard_map/reduce_scatter | solution.py:40
  304.1 144.6 %copy-start.6 = (bf16[2,256,4,128]{1,3,2,0:T(8,128)(2,1)}, bf16[2,256,4,128]{1,3,2,0:T(8,128)(2,1)S(1)}, u32[]{:S(2)}) copy-start(bf16[2,256,4,128]{1,3,2,0:T(8,128)(2,1)S(1)} %copy.103) | copy-start | bytes 1572868
  376.3 72.5 %copy-start.5 = (bf16[2,256,4,128]{1,3,2,0:T(8,128)(2,1)}, bf16[2,256,4,128]{1,3,2,0:T(8,128)(2,1)S(1)}, u32[]{:S(2)}) copy-start(bf16[2,256,4,128]{1,3,2,0:T(8,128)(2,1)S(1)} %copy.100) | copy-start | bytes 1572868
  451.3 69.8 %copy-start.17 = (bf16[1,2,256,4,128]{4,3,2,1,0:T(4,128)(2,1)}, bf16[1,2,256,4,128]{4,3,2,1,0:T(4,128)(2,1)S(1)}, u32[]{:S(2)}) copy-start(bf16[1,2,256,4,128]{4,3,2,1,0:T(4,128)(2,1)S(1)} %copy.89) | copy-start | bytes 1572868
  521.2 46.6 %copy-start.25 = (bf16[128,512]{1,0:T(8,128)(2,1)S(1)}, bf16[128,512]{1,0:T(8,128)(2,1)}, u32[]{:S(2)}) copy-start(bf16[128,512]{1,0:T(8,128)(2,1)} %param.29) | copy-start | bytes 393220
  521.2 170.4 %all-gather.26.cloned.1.call-start = ((), (), s32[]{:S(2)}) async-start(), calls=%async_computation.24 | async-start | bytes 4325376 | tf_op jit(solution)/shard_map/all_gather | solution.py:160
  521.9 242.8 %all-gather.30.cloned.1.call-start = ((), (), s32[]{:S(2)}) async-start(), calls=%async_computation.26 | async-start | bytes 2162688 | tf_op jit(solution)/shard_map/all_gather | solution.py:156
  522.7 271.6 %all-gather.28.cloned.1.call-start = ((), (), s32[]{:S(2)}) async-start(), calls=%async_computation.25 | async-start | bytes 2621440 | tf_op jit(solution)/shard_map/all_gather | solution.py:36
  566.4 3.8 copy-start.39
  566.7 3.5 copy-start.43
  570.2 10.3 copy-start.30
  570.2 65.2 %copy-start.46 = (s32[1,2]{1,0:T(1,128)S(1)}, s32[1,2]{1,0:T(1,128)}, u32[]{:S(2)}) copy-start(s32[1,2]{1,0:T(1,128)} %param.19) | copy-start | bytes 28
  570.2 65.2 %all-to-all-start = ((bf16[32,128,512]{2,1,0:T(8,128)(2,1)}), bf16[32,128,512]{2,1,0:T(8,128)(2,1)}, u32[]{:S(2)}, u32[]{:S(2)}) async-start(bf16[32,128,512]{2,1,0:T(8,128)(2,1)} %stack.2), calls=%async_computation.1 | async-start | bytes 8388608 | tf_op jit(solution)/shard_map/all_to_all | solution.py:158
  579.9 289.7 %all-gather.32.cloned.1.call-start = ((), (), s32[]{:S(2)}) async-start(), calls=%async_computation.27 | async-start | bytes 2162688 | tf_op jit(solution)/shard_map/all_gather | solution.py:161
  580.5 337.9 %reduce-scatter.24.cloned.1.call-start = ((), (), s32[]{:S(2)}) async-start(), calls=%async_computation.28 | async-start | bytes 5242880 | tf_op jit(solution)/shard_map/reduce_scatter | solution.py:40
  635.4 166.5 %copy-start.36 = (pred[2,16]{1,0:T(4,128)(4,1)}, pred[2,16]{1,0:T(4,128)(4,1)S(1)}, u32[]{:S(2)}) copy-start(pred[2,16]{1,0:T(4,128)(4,1)S(1)} %iota_compare_fusion) | copy-start | bytes 100
  874.7 151.5 %all-gather.36.cloned.1.call-start = ((), (), s32[]{:S(2)}) async-start(), calls=%async_computation.30 | async-start | bytes 8650752 | tf_op jit(solution)/shard_map/all_gather | solution.py:162
  875.3 180.1 %all-gather.34.cloned.1.call-start = ((), (), s32[]{:S(2)}) async-start(), calls=%async_computation.29 | async-start | bytes 2621440 | tf_op jit(solution)/shard_map/all_gather | solution.py:36
  922.3 164.6 %all-gather.40.cloned.1.call-start = ((), (), s32[]{:S(2)}) async-start(), calls=%async_computation.33 | async-start | bytes 2621440 | tf_op jit(solution)/shard_map/all_gather | solution.py:44
  922.9 271.9 %all-gather.38.cloned.1.call-start = ((), (), s32[]{:S(2)}) async-start(), calls=%async_computation.31 | async-start | bytes 8650752 | tf_op jit(solution)/shard_map/all_gather | solution.py:163
  923.5 317.3 %reduce-scatter.28.cloned.1.call-start = ((), (), s32[]{:S(2)}) async-start(), calls=%async_computation.34 | async-start | bytes 2621440 | tf_op jit(solution)/shard_map/reduce_scatter | solution.py:48
  1194.8 13.4 copy-start.44
  1214.4 75.0 %reduce-scatter.26.cloned.1.call-start = ((), (), s32[]{:S(2)}) async-start(), calls=%async_computation.32 | async-start | bytes 5242880 | tf_op jit(solution)/shard_map/reduce_scatter | solution.py:40
  1225.0 98.4 %all-gather.42.cloned.1.call-start = ((), (), s32[]{:S(2)}) async-start(), calls=%async_computation.35 | async-start | bytes 2621440 | tf_op jit(solution)/shard_map/all_gather | solution.py:44
  1293.4 76.7 %reduce-scatter.30.cloned.1.call-start = ((), (), s32[]{:S(2)}) async-start(), calls=%async_computation.36 | async-start | bytes 2621440 | tf_op jit(solution)/shard_map/reduce_scatter | solution.py:48
  1340.6 93.0 %all-gather.44.cloned.1.call-start = ((), (), s32[]{:S(2)}) async-start(), calls=%async_computation.37 | async-start | bytes 2621440 | tf_op jit(solution)/shard_map/all_gather | solution.py:44
  1375.1 101.1 %reduce-scatter.34.cloned.1.call-start = ((), (), s32[]{:S(2)}) async-start(), calls=%async_computation.39 | async-start | bytes 327680 | tf_op jit(solution)/shard_map/reduce_scatter | solution.py:223
  1375.4 6.4 copy-start.2
  1376.8 4.9 copy-start.21
  1378.1 5.7 copy-start.19
  1383.8 4.5 copy-start.20
  1383.8 233.2 %reduce-scatter.46.cloned.1.call-start = ((), (), s32[]{:S(2)}) async-start(), calls=%async_computation.45 | async-start | bytes 2162688 | tf_op jit(solution)/shard_map/reduce_scatter | solution.py:290
  1388.3 413.2 %reduce-scatter.44.cloned.1.call-start = ((), (), s32[]{:S(2)}) async-start(), calls=%async_computation.44 | async-start | bytes 2162688 | tf_op jit(solution)/shard_map/reduce_scatter | solution.py:281
  1392.5 609.4 %reduce-scatter.50.cloned.1.call-start = ((), (), s32[]{:S(2)}) async-start(), calls=%async_computation.47 | async-start | bytes 8650752 | tf_op jit(solution)/shard_map/reduce_scatter | solution.py:296
  1402.7 799.2 %reduce-scatter.48.cloned.1.call-start = ((), (), s32[]{:S(2)}) async-start(), calls=%async_computation.46 | async-start | bytes 8650752 | tf_op jit(solution)/shard_map/reduce_scatter | solution.py:293
  1413.0 978.7 %reduce-scatter.54.cloned.1.call-start = ((), (), s32[]{:S(2)}) async-start(), calls=%async_computation.49 | async-start | bytes 4325376
  1422.9 1158.4 %reduce-scatter.52.cloned.1.call-start = ((), (), s32[]{:S(2)}) async-start(), calls=%async_computation.48 | async-start | bytes 4325376
  1433.5 5.6 copy-start.27
  1433.6 5.6 copy-start.32
  1433.6 1332.3 %reduce-scatter.42.cloned.1.call-start = ((), (), s32[]{:S(2)}) async-start(), calls=%async_computation.43 | async-start | bytes 2162688 | tf_op jit(solution)/shard_map/reduce_scatter | solution.py:278
  1438.8 1511.6 %reduce-scatter.38.cloned.1.call-start = ((), (), s32[]{:S(2)}) async-start(), calls=%async_computation.41 | async-start | bytes 2162688 | tf_op jit(solution)/shard_map/reduce_scatter | solution.py:269
  1439.2 5.7 copy-start.14
  1454.0 1680.6 %reduce-scatter.36.cloned.1.call-start = ((), (), s32[]{:S(2)}) async-start(), calls=%async_computation.40 | async-start | bytes 2162688 | tf_op jit(solution)/shard_map/reduce_scatter | solution.py:266
  1458.3 4.4 copy-start.4
  1462.6 2.8 copy-start.9
  1462.6 1697.5 %reduce-scatter.32.cloned.1.call-start = ((), (), s32[]{:S(2)}) async-start(), calls=%async_computation.38 | async-start | bytes 2621440 | tf_op jit(solution)/shard_map/reduce_scatter | solution.py:48
  1465.4 3.1 copy-start.11
  1465.4 3.1 copy-start.15
  1472.7 1884.8 %reduce-scatter.40.cloned.1.call-start = ((), (), s32[]{:S(2)}) async-start(), calls=%async_computation.42 | async-start | bytes 2162688 | tf_op jit(solution)/shard_map/reduce_scatter | solution.py:275
  1475.4 1684.7 %copy-start.1 = (bf16[1,128,2048]{2,1,0:T(8,128)(2,1)S(1)}, bf16[1,128,2048]{2,1,0:T(8,128)(2,1)}, u32[]{:S(2)}) copy-start(bf16[1,128,2048]{2,1,0:T(8,128)(2,1)} %param.17) | copy-start | bytes 1572868
  1475.4 1684.7 %copy-start.24 = (f32[2048]{0:T(1024)S(1)}, f32[2048]{0:T(1024)}, u32[]{:S(2)}) copy-start(f32[2048]{0:T(1024)} %copy-done.23) | copy-start | bytes 24580
  1475.4 1684.7 %copy-start.38 = (f32[128]{0:T(128)S(1)}, f32[128]{0:T(128)}, u32[]{:S(2)}) copy-start(f32[128]{0:T(128)} %copy-done.37) | copy-start | bytes 1540
  1475.4 1684.7 %copy-start.42 = (f32[128]{0:T(128)S(1)}, f32[128]{0:T(128)}, u32[]{:S(2)}) copy-start(f32[128]{0:T(128)} %copy-done.41) | copy-start | bytes 1540
  1475.4 1686.2 %copy-start.33 = (f32[2048]{0:T(1024)S(1)}, f32[2048]{0:T(1024)}, u32[]{:S(2)}) copy-start(f32[2048]{0:T(1024)} %get-tuple-element.64) | copy-start | bytes 24580
  1475.4 1686.2 %copy-start.34 = (f32[2048]{0:T(1024)S(1)}, f32[2048]{0:T(1024)}, u32[]{:S(2)}) copy-start(f32[2048]{0:T(1024)} %get-tuple-element.66) | copy-start | bytes 24580
  1475.4 1883.6 %copy-start.8 = (f32[1,128,2048]{2,1,0:T(8,128)S(1)}, f32[1,128,2048]{2,1,0:T(8,128)}, u32[]{:S(2)}) copy-start(f32[1,128,2048]{2,1,0:T(8,128)} %get-tuple-element.83) | copy-start | bytes 3145732
  (17 other events, 17.6 us)
Sparse Core Ops, SparseCore 0:
  201.9 23.3 all-gather.15
  228.5 71.7 all-gather.19
  303.4 68.9 all-gather.21
  375.4 68.9 all-gather.17
  447.4 68.9 all-gather.23
  521.3 43.5 reduce-scatter.21
  568.5 123.0 all-gather.25
  695.2 69.5 all-gather.29
  767.1 27.1 all-gather.27
  797.8 71.7 all-gather.31
  874.8 43.5 reduce-scatter.23
  921.4 104.7 all-gather.35
  1028.4 26.8 all-gather.33
  1056.8 29.9 all-gather.39
  1089.9 104.8 all-gather.37
  1214.5 26.1 reduce-scatter.27
  1243.1 46.2 reduce-scatter.25
  1293.5 29.8 all-gather.41
  1340.7 29.2 reduce-scatter.29
  1375.3 29.8 all-gather.43
  1408.2 18.2 reduce-scatter.33
  1428.9 187.9 reduce-scatter.45
  1619.5 181.9 reduce-scatter.43
  1803.7 198.1 reduce-scatter.49
  2004.4 197.5 reduce-scatter.47
  2204.2 187.5 reduce-scatter.53
  2394.0 187.2 reduce-scatter.51
  2583.7 182.1 reduce-scatter.41
  2768.4 182.0 reduce-scatter.37
  2952.7 181.8 reduce-scatter.35
  3137.1 22.9 reduce-scatter.31
  3162.5 188.2 reduce-scatter.39
